TPU v7x, 32 devices: a whole 2x2x4 slice. The times are simulated.
32 devices in a mesh: chan: 8 (over z, x), freq: 4 (over y, core).
Axes of the slice: x: 2, y: 2, z: 4, core: 2. Of those that a mesh axis runs over, the one named last changes fastest.
Arguments:
- traces: bfloat16 [1024, 20480], P('chan', 'freq'), may hold values from -2000 to 2000
- kept_bins: int32 [128], replicated, may hold values from 1 to 255, as said below
- round_masks: int32 [2], replicated, may hold values from 1 to 7, as said below
Outputs:
- cross_spectra: float32 [2, 128, 2, 1024, 128], P(None, 'freq', None, 'chan')
- auto_spectra: float32 [128, 2, 1024, 128], P('freq', None, 'chan')
Inputs may be any that keep to these rules, and one draw needn't show every extreme that they name: `kept_bins`: 128 distinct bin numbers in increasing order; 1 and 255 are among them. `round_masks`: 2 distinct numbers; in round r channel block b is paired with block b XOR round_masks[r].
All inputs are finite; a program needn't handle non-finite values.
Results may differ from a plain program's by a relative error of at most 0.0066.
Values may be sent and summed in bfloat16 or wider, within the bound.
A program may use at most 64 MiB of HBM per device.

v0:
```python
import math

import jax
import jax.numpy as jnp
from jax import lax
from jax.sharding import PartitionSpec as P

NS = 512
ROUNDS = 2


EPSILON = 1e-06


def shifted(block, axis, distance):
    devices = range(lax.axis_size(axis))
    route = [(i - distance, i) for i in devices if i - distance in devices]
    return lax.ppermute(block, axis, route)


def swapped(shard, axis, distance):
    return lax.ppermute(shard, axis, [(i, i ^ 1 << distance) for i in range(lax.axis_size(axis))])


def dft_table(kept_bins):
    sample_index = jnp.arange(NS, dtype=jnp.int32)
    phase_index = kept_bins[:, None] * sample_index[None, :] % NS
    angles = phase_index.astype(jnp.float32) * jnp.float32(2.0 * math.pi / NS)
    hann_taper = 0.5 - 0.5 * jnp.cos(
        sample_index.astype(jnp.float32) * jnp.float32(2.0 * math.pi / NS)
    )
    stacked = jnp.stack([hann_taper * jnp.cos(angles), -hann_taper * jnp.sin(angles)], axis=1)
    return stacked.reshape(kept_bins.shape[0] * 2, NS).astype(jnp.bfloat16)


def correlate(left_block, right_block, windows):
    products = jnp.einsum(
        "kpwc,kqwd->kpqcd", left_block, right_block, preferred_element_type=jnp.float32
    )
    real_part = products[:, 0, 0] + products[:, 1, 1]
    imag_part = products[:, 1, 0] - products[:, 0, 1]
    return jnp.stack([real_part, imag_part], axis=1) * (1.0 / math.sqrt(windows))


def body(traces, kept_bins, round_masks):
    channels, samples_here = traces.shape
    hop_length = NS // 2
    frames = samples_here // hop_length
    keep_count = kept_bins.shape[0]
    transform = dft_table(kept_bins)
    following = shifted(traces[:, :hop_length], "freq", -1)
    extended = jnp.concatenate([traces, following], axis=1).reshape(
        channels, frames + 1, hop_length
    )
    spectra = jnp.einsum(
        "kn,cjn->kjc",
        transform[:, :hop_length],
        extended[:, :-1],
        preferred_element_type=jnp.float32,
    )
    spectra = spectra + jnp.einsum(
        "kn,cjn->kjc",
        transform[:, hop_length:],
        extended[:, 1:],
        preferred_element_type=jnp.float32,
    )
    rounded = spectra.astype(jnp.bfloat16).reshape(keep_count, 2, frames * channels)
    windows = frames * lax.axis_size("freq")
    values = rounded.astype(jnp.float32).reshape(keep_count, 2, frames, channels)
    partial_power = jnp.sum(values * values, axis=(1, 2))
    power_mean = lax.psum(partial_power, "freq") / windows
    whitened = (values * lax.rsqrt(power_mean + EPSILON)[:, None, None, :]).astype(jnp.bfloat16)
    arrived_bins = lax.all_to_all(
        whitened.reshape(keep_count, 2, frames * channels),
        "freq",
        split_axis=0,
        concat_axis=2,
        tiled=True,
    )
    own_block = arrived_bins.reshape(-1, 2, windows, channels)
    auto_spectra = correlate(own_block, own_block, windows)
    blocks_count = lax.axis_size("chan")
    crosses = []
    levels = blocks_count.bit_length() - 1
    for round_no in range(ROUNDS):
        round_mask = round_masks[round_no]
        carried = own_block
        for which_bit in range(levels):
            arrived = swapped(carried, "chan", which_bit)
            chosen = jnp.bitwise_and(jnp.right_shift(round_mask, which_bit), 1) == 1
            carried = jnp.where(chosen, arrived, carried)
        crosses.append(correlate(own_block, carried, windows))
    return (jnp.stack(crosses), auto_spectra)


def solution(mesh):
    placed = (P("chan", "freq"), P(), P())
    return jax.shard_map(
        body,
        mesh=mesh,
        in_specs=placed,
        out_specs=(P(None, "freq", None, "chan", None), P("freq", None, "chan", None)),
        check_vma=False,
    )
```

profile of v0, /device:TPU:0, one launch (start us, length us, event | category | flops | bytes accessed | tf_op | source)
XLA Modules:
  0.0 279.2 jit_solution(17597513217299040912)
XLA Ops:
  7.2 1.8 copy.73
  14.4 1.8 convert_bitcast_fusion
  16.2 2.4 copy.77
  18.6 2.5 reshape.399
  21.1 28.2 %all-reduce.2.cloned.1.call-done = f32[128,128]{1,0:T(8,128)} async-done(((f32[128,128]{1,0:T(8,128)}), f32[128,128]{1,0:T(8,128)}) %all-reduce.2.cloned.1.call-update) | async-done | bytes 65552 | tf_op jit(solution)/shard_map/psum | solution.py:71
  51.5 2.8 %copy.80 = f32[128,2560]{1,0:T(8,128)} copy(f32[128,2560]{0,1:T(8,128)} %bitcast.85) | data formatting | bytes 2621440 | tf_op jit(solution)/shard_map/mul | solution.py:72
  54.3 2.7 multiply_convert_fusion
  57.0 19.7 %all_to_all.15 = bf16[128,2,2560]{2,1,0:T(2,128)(2,1)S(1)} all-to-all(bf16[128,2,2560]{2,1,0:T(2,128)(2,1)S(1)} %multiply_convert_fusion), channel_id=1, replica_groups=mesh['chan'=8,'freq'=4] {'freq'}, dimensions={0} | all-to-all | bytes 2621440 | tf_op jit(solution)/shard_map/all_to_all | solution.py:73
  78.2 1.5 collective-permute-start.1
  81.7 26.8 %collective-permute-done.1 = bf16[32,2,80,128]{3,2,1,0:T(8,128)(2,1)S(1)} collective-permute-done((bf16[32,2,80,128]{3,2,1,0:T(8,128)(2,1)S(1)}, bf16[32,2,80,128]{3,2,1,0:T(8,128)(2,1)S(1)}, u32[]{:S(2)}, u32[]{:S(2)}) %collective-permute-start.1) | collective-permute-done | bytes 1310752 | tf_op jit(solution)/shard_map/ppermute | solution.py:22
  108.5 1.7 broadcast_select_fusion.2
  110.1 1.5 collective-permute-start.2
  115.2 26.9 %collective-permute-done.2 = bf16[32,2,80,128]{3,2,1,0:T(8,128)(2,1)} collective-permute-done((bf16[32,2,80,128]{3,2,1,0:T(8,128)(2,1)}, bf16[32,2,80,128]{3,2,1,0:T(8,128)(2,1)}, u32[]{:S(2)}, u32[]{:S(2)}) %collective-permute-start.2) | collective-permute-done | bytes 1310752 | tf_op jit(solution)/shard_map/ppermute | solution.py:22
  142.1 1.5 broadcast_select_fusion.3
  143.6 2.5 collective-permute-start.3
  148.1 46.8 %collective-permute-done.4 = bf16[32,2,80,128]{3,2,1,0:T(8,128)(2,1)S(1)} collective-permute-done((bf16[32,2,80,128]{3,2,1,0:T(8,128)(2,1)}, bf16[32,2,80,128]{3,2,1,0:T(8,128)(2,1)S(1)}, u32[]{:S(2)}, u32[]{:S(2)}) %collective-permute-start.4) | collective-permute-done | bytes 1310752 | tf_op jit(solution)/shard_map/ppermute | solution.py:22
  196.2 2.5 maximum_multiply_fusion.2
  198.6 5.6 %copy.88 = f32[32,2,128,128]{3,2,1,0:T(8,128)} copy(f32[32,2,128,128]{2,3,0,1:T(8,128)} %maximum_multiply_fusion.2) | data formatting | bytes 8388608
  204.2 23.3 %collective-permute-done.3 = bf16[32,2,80,128]{3,2,1,0:T(8,128)(2,1)} collective-permute-done((bf16[32,2,80,128]{3,2,1,0:T(8,128)(2,1)S(1)}, bf16[32,2,80,128]{3,2,1,0:T(8,128)(2,1)}, u32[]{:S(2)}, u32[]{:S(2)}) %collective-permute-start.3) | collective-permute-done | bytes 1310752 | tf_op jit(solution)/shard_map/ppermute | solution.py:22
  227.5 2.6 convolution_bitcast_fusion.2
  230.6 24.2 %collective-permute-done.5 = bf16[32,2,80,128]{3,2,1,0:T(8,128)(2,1)} collective-permute-done((bf16[32,2,80,128]{3,2,1,0:T(8,128)(2,1)}, bf16[32,2,80,128]{3,2,1,0:T(8,128)(2,1)}, u32[]{:S(2)}, u32[]{:S(2)}) %collective-permute-start.5) | collective-permute-done | bytes 1310752 | tf_op jit(solution)/shard_map/ppermute | solution.py:22
  254.8 2.6 convolution_bitcast_fusion.1
  259.7 3.8 %pad_maximum_fusion = f32[2,32,2,128,128]{3,4,1,2,0:T(8,128)} fusion(f32[1,32,2,128,128]{3,4,1,2,0:T(8,128)S(1)} %maximum_multiply_fusion.1, f32[1,32,2,128,128]{3,4,1,2,0:T(8,128)S(1)} %maximum_multiply_fusion), kind=kLoop, calls=%fused_computation | loop fusion | flops 2097152 | bytes 16777216 | tf_op jit(solution)/shard_map/stack | solution.py:93
  263.5 8.9 %copy.87 = f32[2,32,2,128,128]{4,3,2,1,0:T(8,128)} copy(f32[2,32,2,128,128]{3,4,1,2,0:T(8,128)} %pad_maximum_fusion) | data formatting | bytes 16777216
  (41 shorter events, 16.8 us)
Async XLA Ops:
  7.2 3.2 %copy-start.3 = (s32[128]{0:T(128)S(1)}, s32[128]{0:T(128)}, u32[]{:S(2)}) copy-start(s32[128]{0:T(128)} %param.4) | copy-start | bytes 1540
  7.2 42.1 %all-reduce.2.cloned.1.call-start = ((), (), s32[]{:S(2)}) async-start(), calls=%async_computation.1 | async-start | bytes 131072 | tf_op jit(solution)/shard_map/psum | solution.py:71
  9.0 3.1 %collective-permute-start = (bf16[128,256]{0,1:T(8,128)(2,1)S(1)}, bf16[128,256]{0,1:T(8,128)(2,1)S(1)}, u32[]{:S(2)}, u32[]{:S(2)}) collective-permute-start(bf16[128,256]{0,1:T(8,128)(2,1)S(1)} %slice.76), channel_id=1, source_target_pairs={{1,0},{2,1},{3,2},{5,4},{6,5},{7,6},{9,8},{10,9},{11,10},{13,12},{... | collective-permute-start | bytes 196616 | tf_op jit(solution)/shard_map/ppermute | solution.py:18
  50.2 4.1 %copy-start = (f32[128,2,2560]{2,1,0:T(2,128)S(1)}, f32[128,2,2560]{2,1,0:T(2,128)}, u32[]{:S(2)}) copy-start(f32[128,2,2560]{2,1,0:T(2,128)} %reshape.399) | copy-start | bytes 7864324
  76.7 3.1 %copy-start.2 = (s32[2]{0:T(128)S(1)}, s32[2]{0:T(128)}, u32[]{:S(2)}) copy-start(s32[2]{0:T(128)} %param.5) | copy-start | bytes 28
  78.2 30.2 %collective-permute-start.1 = (bf16[32,2,80,128]{3,2,1,0:T(8,128)(2,1)S(1)}, bf16[32,2,80,128]{3,2,1,0:T(8,128)(2,1)S(1)}, u32[]{:S(2)}, u32[]{:S(2)}) collective-permute-start(bf16[32,2,80,128]{3,2,1,0:T(8,128)(2,1)S(1)} %reshape.398), channel_id=1, source_target_pairs={{0,4},{4,0},{8,12},{12,8},{16,20},{20,16},{24,28},{28,24},{1,5},{5... | collective-permute-start | bytes 3932168 | tf_op jit(solution)/shard_map/ppermute | solution.py:22
  110.1 32.0 %collective-permute-start.2 = (bf16[32,2,80,128]{3,2,1,0:T(8,128)(2,1)}, bf16[32,2,80,128]{3,2,1,0:T(8,128)(2,1)}, u32[]{:S(2)}, u32[]{:S(2)}) collective-permute-start(bf16[32,2,80,128]{3,2,1,0:T(8,128)(2,1)} %get-tuple-element.16), channel_id=1, source_target_pairs={{0,8},{4,12},{8,0},{12,4},{16,24},{20,28},{24,16},{28,20},{1,9},{5... | collective-permute-start | bytes 3932168 | tf_op jit(solution)/shard_map/ppermute | solution.py:22
  114.6 80.3 %collective-permute-start.4 = (bf16[32,2,80,128]{3,2,1,0:T(8,128)(2,1)}, bf16[32,2,80,128]{3,2,1,0:T(8,128)(2,1)S(1)}, u32[]{:S(2)}, u32[]{:S(2)}) collective-permute-start(bf16[32,2,80,128]{3,2,1,0:T(8,128)(2,1)} %get-tuple-element.17), channel_id=1, source_target_pairs={{0,8},{4,12},{8,0},{12,4},{16,24},{20,28},{24,16},{28,20},{1,9},{5... | collective-permute-start | bytes 3932168 | tf_op jit(solution)/shard_map/ppermute | solution.py:22
  143.6 83.9 %collective-permute-start.3 = (bf16[32,2,80,128]{3,2,1,0:T(8,128)(2,1)S(1)}, bf16[32,2,80,128]{3,2,1,0:T(8,128)(2,1)}, u32[]{:S(2)}, u32[]{:S(2)}) collective-permute-start(bf16[32,2,80,128]{3,2,1,0:T(8,128)(2,1)S(1)} %broadcast_select_fusion.3), channel_id=1, source_target_pairs={{0,16},{4,20},{8,24},{12,28},{16,0},{20,4},{24,8},{28,12},{1,17},{... | collective-permute-start | bytes 3932168 | tf_op jit(solution)/shard_map/ppermute | solution.py:22
  147.7 47.2 %copy-start.1 = (bf16[32,2,80,128]{3,2,1,0:T(8,128)(2,1)S(1)}, bf16[32,2,80,128]{3,2,1,0:T(8,128)(2,1)}, u32[]{:S(2)}) copy-start(bf16[32,2,80,128]{3,2,1,0:T(8,128)(2,1)} %get-tuple-element.17) | copy-start | bytes 3932164
  196.2 58.6 %collective-permute-start.5 = (bf16[32,2,80,128]{3,2,1,0:T(8,128)(2,1)}, bf16[32,2,80,128]{3,2,1,0:T(8,128)(2,1)}, u32[]{:S(2)}, u32[]{:S(2)}) collective-permute-start(bf16[32,2,80,128]{3,2,1,0:T(8,128)(2,1)} %broadcast_select_fusion.1), channel_id=1, source_target_pairs={{0,16},{4,20},{8,24},{12,28},{16,0},{20,4},{24,8},{28,12},{1,17},{... | collective-permute-start | bytes 3932168 | tf_op jit(solution)/shard_map/ppermute | solution.py:22
Sparse Core Ops, SparseCore 0:
  14.5 34.7 all-reduce.1
where the time goes:
time: 280 us; the launch traced here: 279 us
  waiting for transfers between devices  176 us (63%)
  local copies, waits for them, and re-layouts  28.5 us (10%)
  other arithmetic  21.6 us (8%)
  blocking collectives  19.7 us (7%)
  between operations  18 us (6%)
  matrix products  7.73 us (3%)
  starting transfers between devices  7.43 us (3%)
    ppermute x5, waiting for transfers between devices, swapped(): lax.ppermute(shard, axis, [(i, i ^ 1 << distance) for i in range(lax.axis...  148 us
    psum x1, waiting for transfers between devices, body(): power_mean = lax.psum(partial_power, 'freq') / windows  28.2 us
    all_to_all x1, blocking collectives, body(): lax.all_to_all(whitened.reshape(keep_count, 2, frames * channels), 'freq'...  19.7 us
    unnamed x11, local copies, waits for them, and re-layouts  16.3 us
    dot_general x3, matrix products, correlate(): jnp.einsum('kpwc,kqwd->kpqcd', left_block, right_block, preferred_element...  6.52 us
    ppermute x5, starting transfers between devices, swapped(): lax.ppermute(shard, axis, [(i, i ^ 1 << distance) for i in range(lax.axis...  6.1 us
  transfers between devices with their start and end apart: 7, of which 7 were waited for; matrix products, arithmetic and copies ran while one was open for 9% of the time, Pallas kernels for 0%

commit v1 on v0

v1 whole, which is shorter than its diff:
```python
import functools
import math

import jax
import jax.numpy as jnp
from jax import lax
from jax.experimental import pallas as pl
from jax.experimental.pallas import tpu as pltpu
from jax.sharding import PartitionSpec as P

NS = 512
HOP = NS // 2
EPSILON = 1e-06
PARTS = 2
BINS = 4


def shifted(block, axis, distance):
    devices = range(lax.axis_size(axis))
    route = [(i - distance, i) for i in devices if i - distance in devices]
    return lax.ppermute(block, axis, route)


def moved(pieces, mask):
    route = [(i, i ^ mask) for i in range(lax.axis_size("chan"))]
    return tuple(lax.ppermute(piece, "chan", route) for piece in pieces)


def dft_table(kept_bins):
    sample_index = jnp.arange(NS, dtype=jnp.int32)
    phase_index = kept_bins[:, None] * sample_index[None, :] % NS
    angles = phase_index.astype(jnp.float32) * jnp.float32(2.0 * math.pi / NS)
    hann_taper = 0.5 - 0.5 * jnp.cos(
        sample_index.astype(jnp.float32) * jnp.float32(2.0 * math.pi / NS)
    )
    stacked = jnp.stack([hann_taper * jnp.cos(angles), -hann_taper * jnp.sin(angles)], axis=1)
    return stacked.reshape(kept_bins.shape[0] * 2, NS).astype(jnp.bfloat16)


def nt_dot(a, b):
    return lax.dot_general(a, b, (((1,), (1,)), ((), ())), preferred_element_type=jnp.float32)


def spectra_kernel(frames, traces_ref, following_ref, transform_ref, out_ref, rows):
    count = transform_ref.shape[0]
    for w in range(frames - 1):
        rows[pl.ds(w, count, stride=frames), :] = nt_dot(
            transform_ref[...], traces_ref[:, w * HOP : w * HOP + NS]
        )
    last = nt_dot(transform_ref[:, :HOP], traces_ref[:, (frames - 1) * HOP :])
    last = last + nt_dot(transform_ref[:, HOP:], following_ref[...])
    rows[pl.ds(frames - 1, count, stride=frames), :] = last
    out_ref[...] = rows[...].astype(jnp.bfloat16)


def spectra_of(traces, following, transform):
    channels, samples = traces.shape
    frames = samples // HOP
    shape = (transform.shape[0] * frames, channels)
    return pl.pallas_call(
        functools.partial(spectra_kernel, frames),
        out_shape=jax.ShapeDtypeStruct(shape, jnp.bfloat16),
        in_specs=[pl.BlockSpec(memory_space=pltpu.VMEM)] * 3,
        out_specs=pl.BlockSpec(memory_space=pltpu.VMEM),
        scratch_shapes=[pltpu.VMEM(shape, jnp.float32)],
        compiler_params=pltpu.CompilerParams(vmem_limit_bytes=32 * 2**20),
    )(traces, following, transform)


def correlate_kernel(frames, windows, order_ref, *refs):
    cross_ref, auto_ref = refs[-2:]
    span = 2 * frames
    scale = 1.0 / math.sqrt(windows)
    low_first = order_ref[0]
    blocks = [
        [ref[s].astype(jnp.float32) for ref in refs[at : at + PARTS] for s in range(ref.shape[0])]
        for at in range(0, 3 * PARTS, PARTS)
    ]
    row = lax.broadcasted_iota(jnp.int32, (span, 1), 0)
    sign = jnp.where(row < frames, 1.0, -1.0).astype(jnp.float32)
    for b in range(BINS):
        whitened = []
        for block in blocks:
            values = [part[b * span : (b + 1) * span] for part in block]
            power = sum(jnp.sum(v * v, axis=0, keepdims=True) for v in values) / windows
            gain = lax.rsqrt(power + EPSILON)
            whitened.append([v * gain for v in values])
        left = jnp.concatenate(
            [
                jnp.concatenate([v, pltpu.roll(v, frames, 0) * sign], axis=1)
                for v in whitened[0]
            ],
            axis=0,
        ).astype(jnp.bfloat16)
        right = jnp.concatenate(
            [jnp.concatenate(columns, axis=1) for columns in zip(*whitened)], axis=0
        ).astype(jnp.bfloat16)
        product = scale * lax.dot_general(
            left, right, (((0,), (0,)), ((), ())), preferred_element_type=jnp.float32
        )
        channels = product.shape[0] // 2
        for p in range(2):
            half = product[p * channels : (p + 1) * channels]
            auto_ref[b, p] = half[:, :channels]
            cross_ref[low_first, b, p] = half[:, channels : 2 * channels]
            cross_ref[1 - low_first, b, p] = half[:, 2 * channels :]


def correlate(order, own, low, high, frames, windows):
    sources, rows, channels = own[0].shape
    span = 2 * frames
    bins = rows // span
    in_spec = pl.BlockSpec((sources, BINS * span, channels), lambda i, order: (0, i, 0))
    return pl.pallas_call(
        functools.partial(correlate_kernel, frames, windows),
        grid_spec=pltpu.PrefetchScalarGridSpec(
            num_scalar_prefetch=1,
            grid=(bins // BINS,),
            in_specs=[in_spec] * (3 * PARTS),
            out_specs=[
                pl.BlockSpec((2, BINS, 2, channels, channels), lambda i, order: (0, i, 0, 0, 0)),
                pl.BlockSpec((BINS, 2, channels, channels), lambda i, order: (i, 0, 0, 0)),
            ],
        ),
        out_shape=[
            jax.ShapeDtypeStruct((2, bins, 2, channels, channels), jnp.float32),
            jax.ShapeDtypeStruct((bins, 2, channels, channels), jnp.float32),
        ],
        compiler_params=pltpu.CompilerParams(vmem_limit_bytes=40 * 2**20),
    )(order, *own, *low, *high)


def pair_exchange(low_mask, high_mask, pieces):
    blocks = lax.axis_size("chan")

    def branch(low, high, pieces):
        half = blocks // 2
        if low & half and high & half:
            if low.bit_count() <= high.bit_count():
                first = moved(pieces, low)
                return first, moved(first, low ^ high)
            first = moved(pieces, high)
            return moved(first, low ^ high), first
        return moved(pieces, low), moved(pieces, high)

    pairs = [(a, b) for a in range(1, blocks) for b in range(a + 1, blocks)]
    index = (low_mask - 1) * (blocks - 1) - low_mask * (low_mask - 1) // 2
    index = index + high_mask - low_mask - 1
    return lax.switch(index, [functools.partial(branch, a, b) for a, b in pairs], pieces)


def mask_exchange(mask, pieces):
    blocks = lax.axis_size("chan")
    branches = [lambda pieces, m=m: moved(pieces, m) for m in range(1, blocks)]
    return lax.switch(mask - 1, branches, pieces)


def body(traces, kept_bins, round_masks):
    frames = traces.shape[1] // HOP
    ranks = lax.axis_size("freq")
    following = shifted(traces[:, :HOP], "freq", -1)
    spectra = spectra_of(traces, following, dft_table(kept_bins))
    arrived = lax.all_to_all(spectra, "freq", split_axis=0, concat_axis=0, tiled=True)
    arrived = arrived.reshape(ranks, -1, arrived.shape[1])
    step = ranks // PARTS
    own = tuple(arrived[i * step : (i + 1) * step] for i in range(PARTS))
    low_mask = jnp.minimum(round_masks[0], round_masks[1])
    high_mask = jnp.maximum(round_masks[0], round_masks[1])
    if lax.axis_size("chan") <= 8:
        low, high = pair_exchange(low_mask, high_mask, own)
    else:
        low, high = mask_exchange(low_mask, own), mask_exchange(high_mask, own)
    order = (round_masks[:1] > round_masks[1:]).astype(jnp.int32)
    cross, auto = correlate(order, own, low, high, frames, frames * ranks)
    return cross, auto


def solution(mesh):
    placed = (P("chan", "freq"), P(), P())
    return jax.shard_map(
        body,
        mesh=mesh,
        in_specs=placed,
        out_specs=(P(None, "freq", None, "chan", None), P("freq", None, "chan", None)),
        check_vma=False,
    )
```

time: 280 us -> 103 us (0.37)
  waiting for transfers between devices: 176 us -> 68.4 us
  local copies, waits for them, and re-layouts: 28.5 us -> 2 us
  blocking collectives: 19.7 us -> 0 us
  other arithmetic: 21.6 us -> 1.99 us
  between operations: 18 us -> 4.34 us
  Pallas kernels: 0 us -> 12.3 us
  matrix products: 7.73 us -> 0 us
  starting transfers between devices: 7.43 us -> 13.2 us
    ppermute x5 -> x4, waiting for transfers between devices: 148 us -> 54.9 us  [moved(): return tuple((lax.ppermute(piece, 'chan', route) for piece in pieces))]
    psum x1 -> x0, waiting for transfers between devices: 28.2 us -> none  [body(): power_mean = lax.psum(partial_power, 'freq') / windows]
    all_to_all x1 -> x0, blocking collectives: 19.7 us -> none  [body(): lax.all_to_all(whitened.reshape(keep_count, 2, frames * channels), 'freq'...]
    unnamed x11 -> x4, local copies, waits for them, and re-layouts: 16.3 us -> 0.01 us
    all_to_all x0 -> x1, waiting for transfers between devices: none -> 13.5 us  [body(): lax.all_to_all(spectra, 'freq', split_axis=0, concat_axis=0, tiled=True)]
    pallas_call x0 -> x2, Pallas kernels: none -> 12.3 us  [the longest x1 9.63 us: correlate(): pl.pallas_call(functools.partial(correlate_kernel, frames, windows), grid...]
    dot_general x5 -> x0, matrix products: 7.73 us -> none  [the longest x3 6.52 us: correlate(): jnp.einsum('kpwc,kqwd->kpqcd', left_block, right_block, preferred_element...]
    all_to_all x0 -> x1, starting transfers between devices: none -> 5.1 us  [body(): lax.all_to_all(spectra, 'freq', split_axis=0, concat_axis=0, tiled=True)]
  transfers between devices with their start and end apart: 7 -> 6, of which waited for: 7 -> 4; matrix products, arithmetic and copies ran while one was open for 9% -> 3% of each run, Pallas kernels for 0% -> 0%
where the time goes in v1:
time: 103 us; the launch traced here: 102 us
  waiting for transfers between devices  68.4 us (66%)
  starting transfers between devices  13.2 us (13%)
  Pallas kernels  12.3 us (12%)
  between operations  4.34 us (4%)
  local copies, waits for them, and re-layouts  2 us (2%)
  other arithmetic  1.99 us (2%)
    ppermute x4, waiting for transfers between devices, moved(): return tuple((lax.ppermute(piece, 'chan', route) for piece in pieces))  54.9 us
    all_to_all x1, waiting for transfers between devices, body(): lax.all_to_all(spectra, 'freq', split_axis=0, concat_axis=0, tiled=True)  13.5 us
    pallas_call x1, Pallas kernels, correlate(): pl.pallas_call(functools.partial(correlate_kernel, frames, windows), grid...  9.63 us
    ppermute x4, starting transfers between devices, moved(): return tuple((lax.ppermute(piece, 'chan', route) for piece in pieces))  6.81 us
    all_to_all x1, starting transfers between devices, body(): lax.all_to_all(spectra, 'freq', split_axis=0, concat_axis=0, tiled=True)  5.1 us
    pallas_call x1, Pallas kernels, spectra_of(): pl.pallas_call(functools.partial(spectra_kernel, frames), out_shape=jax.S...  2.67 us
  transfers between devices with their start and end apart: 6, of which 4 were waited for; matrix products, arithmetic and copies ran while one was open for 3% of the time, Pallas kernels for 0%

profile of v1, /device:TPU:0, one launch (start us, length us, event | category | flops | bytes accessed | tf_op | source)
XLA Modules:
  0.0 102.3 jit_solution(8492785594180834883)
XLA Ops:
  0.6 0.0 copy-start
  0.6 0.9 slice.25
  1.6 1.3 %collective-permute-start.84 = (bf16[128,256]{1,0:T(8,128)(2,1)S(1)}, bf16[128,256]{1,0:T(8,128)(2,1)S(1)}, u32[]{:S(2)}, u32[]{:S(2)}) collective-permute-start(bf16[128,256]{1,0:T(8,128)(2,1)S(1)} %slice.25), channel_id=1, source_target_pairs={{1,0},{2,1},{3,2},{5,4},{6,5},{7,6},{9,8},{10,9},{11,10},{13,12},{... | collective-permute-start | bytes 196616 | tf_op jit(solution)/shard_map/ppermute | solution.py:21
  2.9 1.9 %multiply_convert_fusion.1 = (bf16[128,1,512]{2,0,1:T(8,128)(2,1)S(1)}, bf16[128,1,512]{2,0,1:T(8,128)(2,1)S(1)}) fusion(s32[128]{0:T(128)} %param.25, f32[512]{0:T(512)S(1)} %get-tuple-element.142, f32[512]{0:T(512)S(1)} %get-tuple-element.143), kind=kLoop, calls=%fused_computation.8 | loop fusion | flops 1179648 | bytes 266752 | tf_op jit(solution)/shard_map/convert
  4.9 0.3 copy.5
  5.2 0.1 convert_element_type.35.transform_ref
  5.3 0.0 collective-permute-done.84.following_ref
  5.3 0.0 copy-done
  5.3 2.7 %shard_map.50 = bf16[5120,128]{1,0:T(8,128)(2,1)} custom-call(bf16[128,5120]{1,0:T(8,128)(2,1)S(1)} %copy-done, bf16[128,256]{1,0:T(8,128)(2,1)S(1)} %collective-permute-done.84.following_ref, bf16[256,512]{1,0:T(8,128)(2,1)S(1)} %convert_element_type.35.transform_ref), custom_call_target="tpu_custom_call" | custom-call | tf_op jit(solution)/shard_map/pallas_call | solution.py:60
  8.0 5.1 %all-to-all-start = ((bf16[4,1280,128]{2,1,0:T(8,128)(2,1)}), bf16[4,1280,128]{2,1,0:T(8,128)(2,1)S(1)}, u32[]{:S(2)}, u32[]{:S(2)}) async-start(bf16[4,1280,128]{2,1,0:T(8,128)(2,1)} %bitcast), calls=%async_computation | async-start | bytes 2621440 | tf_op jit(solution)/shard_map/all_to_all | solution.py:163
  13.1 0.0 copy-done.1
  13.1 0.6 fusion.8
  17.3 13.5 %all-to-all-done = bf16[4,1280,128]{2,1,0:T(8,128)(2,1)S(1)} async-done(((bf16[4,1280,128]{2,1,0:T(8,128)(2,1)}), bf16[4,1280,128]{2,1,0:T(8,128)(2,1)S(1)}, u32[]{:S(2)}, u32[]{:S(2)}) %all-to-all-start) | async-done | bytes 1310752 | tf_op jit(solution)/shard_map/all_to_all | solution.py:163
  30.8 0.1 fusion.7
  30.9 61.8 %conditional.1 = (bf16[2,1280,128]{2,1,0:T(8,128)(2,1)}, bf16[2,1280,128]{2,1,0:T(8,128)(2,1)}, bf16[2,1280,128]{2,1,0:T(8,128)(2,1)}, bf16[2,1280,128]{2,1,0:T(8,128)(2,1)}) conditional(s32[]{:T(128)} %clamp.3, (bf16[2,1280,128]{2,1,0:T(8,128)(2,1)S(1)}, bf16[2,1280,128]{2,1,0:T(8,128)(2,1)S(1)}) %tuple.91, ...), branch_computations={%region_0.1_spmd, %region_1.2_spmd, %region_2.3_spmd, %region_3.4_... | conditional | bytes 10485952 | solution.py:149
  30.9 4.6 %collective-permute-start.22 = (bf16[2,1280,128]{2,1,0:T(8,128)(2,1)S(1)}, bf16[2,1280,128]{2,1,0:T(8,128)(2,1)}, u32[]{:S(2)}, u32[]{:S(2)}) collective-permute-start(bf16[2,1280,128]{2,1,0:T(8,128)(2,1)S(1)} %get-tuple-element.94), channel_id=1, source_target_pairs={{0,28},{4,24},{8,20},{12,16},{16,12},{20,8},{24,4},{28,0},{1,29},{... | collective-permute-start | bytes 1966088 | tf_op jit(solution)/shard_map/cond/branch_5_fun/ppermute | solution.py:26
  35.5 0.5 collective-permute-start.20
  36.1 1.1 %collective-permute-start.23 = (bf16[2,1280,128]{2,1,0:T(8,128)(2,1)S(1)}, bf16[2,1280,128]{2,1,0:T(8,128)(2,1)}, u32[]{:S(2)}, u32[]{:S(2)}) collective-permute-start(bf16[2,1280,128]{2,1,0:T(8,128)(2,1)S(1)} %get-tuple-element.95), channel_id=1, source_target_pairs={{0,28},{4,24},{8,20},{12,16},{16,12},{20,8},{24,4},{28,0},{1,29},{... | collective-permute-start | bytes 1966088 | tf_op jit(solution)/shard_map/cond/branch_5_fun/ppermute | solution.py:26
  37.2 0.5 collective-permute-start.21
  37.7 13.9 %collective-permute-done.22 = bf16[2,1280,128]{2,1,0:T(8,128)(2,1)} collective-permute-done((bf16[2,1280,128]{2,1,0:T(8,128)(2,1)S(1)}, bf16[2,1280,128]{2,1,0:T(8,128)(2,1)}, u32[]{:S(2)}, u32[]{:S(2)}) %collective-permute-start.22) | collective-permute-done | bytes 655392 | tf_op jit(solution)/shard_map/cond/branch_5_fun/ppermute | solution.py:26
  51.6 27.1 %collective-permute-done.20 = bf16[2,1280,128]{2,1,0:T(8,128)(2,1)} collective-permute-done((bf16[2,1280,128]{2,1,0:T(8,128)(2,1)S(1)}, bf16[2,1280,128]{2,1,0:T(8,128)(2,1)}, u32[]{:S(2)}, u32[]{:S(2)}) %collective-permute-start.20) | collective-permute-done | bytes 655392 | tf_op jit(solution)/shard_map/cond/branch_5_fun/ppermute | solution.py:26
  78.7 0.0 collective-permute-done.23
  78.7 13.9 %collective-permute-done.21 = bf16[2,1280,128]{2,1,0:T(8,128)(2,1)} collective-permute-done((bf16[2,1280,128]{2,1,0:T(8,128)(2,1)S(1)}, bf16[2,1280,128]{2,1,0:T(8,128)(2,1)}, u32[]{:S(2)}, u32[]{:S(2)}) %collective-permute-start.21) | collective-permute-done | bytes 655392 | tf_op jit(solution)/shard_map/cond/branch_5_fun/ppermute | solution.py:26
  92.7 9.6 %shard_map.51 = (f32[2,32,2,128,128]{4,3,2,1,0:T(8,128)}, f32[32,2,128,128]{3,2,1,0:T(8,128)}) custom-call(s32[1]{0:T(128)S(6)} %convert_element_type.32.order_ref, bf16[2,1280,128]{2,1,0:T(8,128)(2,1)S(1)} %get-tuple-element.137.refs_0_, bf16[2,1280,128]{2,1,0:T(8,128)(2,1)S(1)} %get-tuple-element.136.refs_1_, ...), custom_call_target="tpu_custom_call" | custom-call | tf_op jit(solution)/shard_map/pallas_call | solution.py:114
  (3 shorter events, 0.1 us)
Async XLA Ops:
  0.6 4.7 %copy-start = (bf16[128,5120]{1,0:T(8,128)(2,1)S(1)}, bf16[128,5120]{1,0:T(8,128)(2,1)}, u32[]{:S(2)}) copy-start(bf16[128,5120]{1,0:T(8,128)(2,1)} %traces_ref.1) | copy-start | bytes 3932164
  1.6 3.7 %collective-permute-start.84 = (bf16[128,256]{1,0:T(8,128)(2,1)S(1)}, bf16[128,256]{1,0:T(8,128)(2,1)S(1)}, u32[]{:S(2)}, u32[]{:S(2)}) collective-permute-start(bf16[128,256]{1,0:T(8,128)(2,1)S(1)} %slice.25), channel_id=1, source_target_pairs={{1,0},{2,1},{3,2},{5,4},{6,5},{7,6},{9,8},{10,9},{11,10},{13,12},{... | collective-permute-start | bytes 196616 | tf_op jit(solution)/shard_map/ppermute | solution.py:21
  8.0 5.1 %copy-start.1 = (s32[2]{0:T(128)S(1)}, s32[2]{0:T(128)}, u32[]{:S(2)}) copy-start(s32[2]{0:T(128)} %param.26) | copy-start | bytes 28
  8.0 22.8 %all-to-all-start = ((bf16[4,1280,128]{2,1,0:T(8,128)(2,1)}), bf16[4,1280,128]{2,1,0:T(8,128)(2,1)S(1)}, u32[]{:S(2)}, u32[]{:S(2)}) async-start(bf16[4,1280,128]{2,1,0:T(8,128)(2,1)} %bitcast), calls=%async_computation | async-start | bytes 2621440 | tf_op jit(solution)/shard_map/all_to_all | solution.py:163
  30.9 20.7 %collective-permute-start.22 = (bf16[2,1280,128]{2,1,0:T(8,128)(2,1)S(1)}, bf16[2,1280,128]{2,1,0:T(8,128)(2,1)}, u32[]{:S(2)}, u32[]{:S(2)}) collective-permute-start(bf16[2,1280,128]{2,1,0:T(8,128)(2,1)S(1)} %get-tuple-element.94), channel_id=1, source_target_pairs={{0,28},{4,24},{8,20},{12,16},{16,12},{20,8},{24,4},{28,0},{1,29},{... | collective-permute-start | bytes 1966088 | tf_op jit(solution)/shard_map/cond/branch_5_fun/ppermute | solution.py:26
  35.5 43.2 %collective-permute-start.20 = (bf16[2,1280,128]{2,1,0:T(8,128)(2,1)S(1)}, bf16[2,1280,128]{2,1,0:T(8,128)(2,1)}, u32[]{:S(2)}, u32[]{:S(2)}) collective-permute-start(bf16[2,1280,128]{2,1,0:T(8,128)(2,1)S(1)} %get-tuple-element.94), channel_id=1, source_target_pairs={{0,4},{4,0},{8,12},{12,8},{16,20},{20,16},{24,28},{28,24},{1,5},{5... | collective-permute-start | bytes 1966088 | tf_op jit(solution)/shard_map/cond/branch_5_fun/ppermute | solution.py:26
  36.1 42.7 %collective-permute-start.23 = (bf16[2,1280,128]{2,1,0:T(8,128)(2,1)S(1)}, bf16[2,1280,128]{2,1,0:T(8,128)(2,1)}, u32[]{:S(2)}, u32[]{:S(2)}) collective-permute-start(bf16[2,1280,128]{2,1,0:T(8,128)(2,1)S(1)} %get-tuple-element.95), channel_id=1, source_target_pairs={{0,28},{4,24},{8,20},{12,16},{16,12},{20,8},{24,4},{28,0},{1,29},{... | collective-permute-start | bytes 1966088 | tf_op jit(solution)/shard_map/cond/branch_5_fun/ppermute | solution.py:26
  37.2 55.5 %collective-permute-start.21 = (bf16[2,1280,128]{2,1,0:T(8,128)(2,1)S(1)}, bf16[2,1280,128]{2,1,0:T(8,128)(2,1)}, u32[]{:S(2)}, u32[]{:S(2)}) collective-permute-start(bf16[2,1280,128]{2,1,0:T(8,128)(2,1)S(1)} %get-tuple-element.95), channel_id=1, source_target_pairs={{0,4},{4,0},{8,12},{12,8},{16,20},{20,16},{24,28},{28,24},{1,5},{5... | collective-permute-start | bytes 1966088 | tf_op jit(solution)/shard_map/cond/branch_5_fun/ppermute | solution.py:26
